TPU v7x, 32 devices: a whole 2x2x4 slice. The times are simulated.
32 devices in a mesh: groups: 2 (over y), dp: 4 (over z), tensor: 2 (over x), sub: 2 (over core).
Axes of the slice: x: 2, y: 2, z: 4, core: 2. Of those that a mesh axis runs over, the one named last changes fastest.
Arguments:
- val_hidden: bfloat16 [1024, 7168], P(('groups', 'dp', 'sub'), 'tensor'), parts along dimension 0, may hold values from -6 to 6
- val_cotan: bfloat16 [1024, 4096], P(('groups', 'dp', 'sub')), parts along dimension 0, may hold values from -6 to 6
- val_count: int32 [16], P(('groups', 'dp', 'sub')), parts along dimension 0, may hold values from 16 to 64, as said below
- train_hidden: bfloat16 [2048, 7168], P(('groups', 'dp', 'sub'), 'tensor'), parts along dimension 0, may hold values from -6 to 6
- train_cotan: bfloat16 [2048, 4096], P(('groups', 'dp', 'sub')), parts along dimension 0, may hold values from -6 to 6
- seq_len: int32 [32], P('groups'), parts along dimension 0, may hold values from 1 to 64, as said below
- seq_device: int32 [32], P('groups'), parts along dimension 0, may hold values from 0 to 7, as said below
Outputs:
- weighted_grad: bfloat16 [14336, 4096], P(('groups', 'tensor'), ('dp', 'sub')), parts along dimension 0
- seq_weight: float32 [32], P('groups'), parts along dimension 0
There are 2 independent parts, one for each index of `groups`. A program takes and returns all parts, laid end to end along the dimension named above; each array names one. Nothing has to cross between parts.
Inputs may be any that keep to these rules, and one draw needn't show every extreme that they name: `val_count`: the first data device has 16 live slots and the last data device has all 64 slots live. `seq_len`: the sequences of one device fill at most 128 slots; some device holds 2 sequences of length 64. `seq_device`: every data device holds exactly 2 sequences.
All inputs are finite; a program needn't handle non-finite values.
Results may differ from a plain program's by a relative error of at most 0.0046.
The roundings to bfloat16 on the way count: a program that leaves them out, or rounds other values in their place, can miss the bound.
Values may be sent and summed in bfloat16 or wider, within the bound.
A program may use at most 64 MiB of HBM per device.

v0:
```python
import jax
import jax.numpy as jnp
from jax import lax
from jax.sharding import PartitionSpec as P

D = 4096
FF = 7168


def membership(seq_len, seq_device, row_count, capacity):
    seq_order = jnp.arange(seq_len.shape[0], dtype=jnp.int32)
    shared = seq_device[:, None] == seq_device[None, :]
    earlier = seq_order[None, :] < seq_order[:, None]
    offset = jnp.sum(jnp.where(shared & earlier, seq_len[None, :], 0), axis=1)
    row_ids = jnp.arange(row_count, dtype=jnp.int32)
    holder = row_ids // capacity
    within = row_ids % capacity
    inside = (
        (seq_device[None, :] == holder[:, None])
        & (within[:, None] >= offset[None, :])
        & (within[:, None] < (offset + seq_len)[None, :])
    )
    return inside.astype(jnp.float32)


def shards(val_hidden, val_cotan, val_count, train_hidden, train_cotan, seq_len, seq_device):
    contract_rows = (((0,), (0,)), ((), ()))
    val_slots = val_hidden.shape[0]
    val_live = jnp.arange(val_slots, dtype=jnp.int32) < val_count[0]
    val_kept = jnp.where(val_live[:, None], val_hidden, jnp.zeros_like(val_hidden))
    val_columns, train_columns = (
        lax.all_to_all(val_cotan, ("dp", "sub"), split_axis=1, concat_axis=0, tiled=True),
        lax.all_to_all(train_cotan, ("dp", "sub"), split_axis=1, concat_axis=0, tiled=True),
    )
    val_every, train_every = (
        lax.all_gather(val_kept, ("dp", "sub"), axis=0, tiled=True),
        lax.all_gather(train_hidden, ("dp", "sub"), axis=0, tiled=True),
    )
    val_block = lax.dot_general(
        val_every, val_columns, contract_rows, preferred_element_type=jnp.float32
    )
    val_grad = val_block.astype(jnp.bfloat16)
    projected = jnp.dot(train_every, val_grad, preferred_element_type=jnp.float32)
    token_part = jnp.sum(projected * train_columns, axis=1)
    member = membership(seq_len, seq_device, train_every.shape[0], train_hidden.shape[0])
    part_align = jnp.dot(token_part, member, precision=lax.Precision.HIGHEST)
    count_local = val_count[0].astype(jnp.float32)
    val_total = lax.psum(count_local, ("dp", "sub"))
    align = lax.psum(part_align, ("dp", "tensor", "sub"))
    lengths = seq_len.astype(jnp.float32)
    score = align / jnp.sqrt(val_total * lengths * float(FF) * float(D))
    seq_weight = jax.nn.sigmoid(score)
    mass = jnp.sum(seq_weight * lengths)
    row_weight = jnp.dot(member, seq_weight, precision=lax.Precision.HIGHEST)
    weighted_cotan = (row_weight[:, None] * train_columns).astype(jnp.bfloat16)
    weighted = lax.dot_general(
        train_every, weighted_cotan, contract_rows, preferred_element_type=jnp.float32
    )
    weighted_grad = (weighted / jnp.sqrt(mass)).astype(jnp.bfloat16)
    return (weighted_grad, seq_weight)


def solution(mesh):
    return jax.shard_map(
        shards,
        mesh=mesh,
        in_specs=(
            P(("groups", "dp", "sub"), "tensor"),
            P(("groups", "dp", "sub"), None),
            P(("groups", "dp", "sub")),
            P(("groups", "dp", "sub"), "tensor"),
            P(("groups", "dp", "sub"), None),
            P("groups"),
            P("groups"),
        ),
        out_specs=(P(("groups", "tensor"), ("dp", "sub")), P("groups")),
        check_vma=False,
    )
```

profile of v0, /device:TPU:0, one launch (start us, length us, event | category | flops | bytes accessed | tf_op | source)
XLA Modules:
  0.0 231.7 jit_solution(12047744341904695969)
XLA Ops:
  7.2 0.0 copy-start
  7.2 0.0 all-gather.3.cloned.1.call-start
  7.9 1.9 broadcast_select_fusion
  9.8 0.0 all-gather.3.cloned.1.call-update
  9.8 0.0 copy-start.1
  9.9 0.0 copy-start.2
  9.9 0.0 all-gather.5.cloned.1.call-start
  9.9 0.7 all-gather.5.cloned.1.call-update
  10.6 2.3 copy.22
  12.9 6.3 %all-to-all-start.1 = ((bf16[128,8,512]{0,2,1:T(8,128)(2,1)}), bf16[128,8,512]{0,2,1:T(8,128)(2,1)S(1)}, u32[]{:S(2)}, u32[]{:S(2)}) async-start(bf16[128,8,512]{0,2,1:T(8,128)(2,1)} %bitcast.4), calls=%async_computation.1 | async-start | bytes 2097152 | tf_op jit(solution)/shard_map/all_to_all | solution.py:33
  19.2 0.0 copy-done
  19.2 0.8 copy.28
  20.1 51.4 %all-to-all-done.1 = bf16[128,8,512]{0,2,1:T(8,128)(2,1)S(1)} async-done(((bf16[128,8,512]{0,2,1:T(8,128)(2,1)}), bf16[128,8,512]{0,2,1:T(8,128)(2,1)S(1)}, u32[]{:S(2)}, u32[]{:S(2)}) %all-to-all-start.1) | async-done | bytes 1048608 | tf_op jit(solution)/shard_map/all_to_all | solution.py:33
  71.5 3.5 %all-to-all-start = ((bf16[64,8,512]{2,0,1:T(8,128)(2,1)}), bf16[64,8,512]{2,0,1:T(8,128)(2,1)S(1)}, u32[]{:S(2)}, u32[]{:S(2)}) async-start(bf16[64,8,512]{2,0,1:T(8,128)(2,1)} %bitcast.29), calls=%async_computation | async-start | bytes 1048576 | tf_op jit(solution)/shard_map/all_to_all | solution.py:32
  75.0 0.0 copy-done.1
  75.0 0.0 copy-done.2
  75.0 0.2 select_reduce_fusion
  75.2 1.5 convert_bitcast_fusion
  76.7 1.9 copy.23
  78.6 1.8 copy.24
  80.4 13.4 %all-to-all-done = bf16[64,8,512]{2,0,1:T(8,128)(2,1)S(1)} async-done(((bf16[64,8,512]{2,0,1:T(8,128)(2,1)}), bf16[64,8,512]{2,0,1:T(8,128)(2,1)S(1)}, u32[]{:S(2)}, u32[]{:S(2)}) %all-to-all-start) | async-done | bytes 524320 | tf_op jit(solution)/shard_map/all_to_all | solution.py:32
  93.8 0.0 all-gather.3.cloned.1.call-done
  93.8 57.7 %all-gather.5.cloned.1.call-done = bf16[1024,3584]{1,0:T(8,128)(2,1)} async-done(((bf16[128,3584]{1,0:T(8,128)(2,1)}), bf16[1024,3584]{1,0:T(8,128)(2,1)}) %all-gather.5.cloned.1.call-update) | async-done | bytes 7340048 | tf_op jit(solution)/shard_map/all_gather | solution.py:37
  151.4 10.6 %fusion.1 = f32[1024]{0:T(1024)S(1)} fusion(f32[1024,512]{0,1:T(8,128)} %copy.24, bf16[1024,3584]{1,0:T(8,128)(2,1)} %all-gather.5.cloned.1.call-done, bf16[512,3584]{1,0:T(8,128)(2,1)} %all-gather.3.cloned.1.call-done, bf16[512,512]{1,0:T(8,128)(2,1)S(1)} %bitcast.35), kind=kOutput, calls=%fused_computation.4 | convolution fusion | flops 5640027136 | bytes 13635584 | tf_op jit(solution)/shard_map/dot_general | solution.py:43
  162.1 0.5 convolution_bitcast_fusion
  162.6 15.1 %psum.15 = f32[]{:T(128)} all-reduce(f32[]{:T(128)S(6)} %convert_element_type.33), channel_id=1, replica_groups=mesh['groups'=2,'dp'=4,'tensor'=2,'sub'=2] {'dp','sub'}, use_global_device_ids=true, to_apply=%region_3.4 | all-reduce | flops 1 | bytes 8 | tf_op jit(solution)/shard_map/psum | solution.py:48
  177.7 29.9 %psum.14 = f32[16]{0:T(128)S(1)} all-reduce(f32[16]{0:T(128)S(1)} %convolution_bitcast_fusion), channel_id=1, replica_groups=mesh['groups'=2,'dp'=4,'tensor'=2,'sub'=2] {'dp','tensor','sub'}, use_global_device_ids=true, to_apply=%region_2.3 | all-reduce | flops 16 | bytes 128 | tf_op jit(solution)/shard_map/psum | solution.py:49
  207.6 1.3 multiply_reduce_fusion
  208.9 0.0 copy-start.3
  209.6 0.6 fusion.3
  210.2 8.8 %fusion = bf16[3584,512]{0,1:T(8,128)(2,1)} fusion(bf16[1024,3584]{1,0:T(8,128)(2,1)} %all-gather.5.cloned.1.call-done, f32[]{:T(128)S(6)} %sqrt.7, f32[1024,512]{1,0:T(8,128)S(1)} %bitcast.33, f32[1024]{0:T(1024)S(1)} %bitcast.36), kind=kOutput, calls=%fused_computation.2 | convolution fusion | flops 3762814976 | bytes 13111300 | tf_op jit(solution)/shard_map/dot_general | solution.py:56
  219.0 0.0 copy-done.3
  219.0 5.9 %copy.25 = bf16[3584,512]{1,0:T(8,128)(2,1)} copy(bf16[3584,512]{0,1:T(8,128)(2,1)} %fusion) | data formatting | bytes 7340032
  (3 shorter events, 0.0 us)
Async XLA Ops:
  7.2 12.0 %copy-start = (bf16[64,4096]{1,0:T(8,128)(2,1)S(1)}, bf16[64,4096]{1,0:T(8,128)(2,1)}, u32[]{:S(2)}) copy-start(bf16[64,4096]{1,0:T(8,128)(2,1)} %param.8) | copy-start | bytes 1572868
  7.2 86.6 %all-gather.3.cloned.1.call-start = ((), (), s32[]{:S(2)}) async-start(), calls=%async_computation.2 | async-start | bytes 4128768 | tf_op jit(solution)/shard_map/all_gather | solution.py:36
  9.8 65.2 %copy-start.1 = (s32[16]{0:T(128)S(1)}, s32[16]{0:T(128)}, u32[]{:S(2)}) copy-start(s32[16]{0:T(128)} %param.12) | copy-start | bytes 196
  9.9 65.2 %copy-start.2 = (s32[16]{0:T(128)S(1)}, s32[16]{0:T(128)}, u32[]{:S(2)}) copy-start(s32[16]{0:T(128)} %param.13) | copy-start | bytes 196
  9.9 141.6 %all-gather.5.cloned.1.call-start = ((), (), s32[]{:S(2)}) async-start(), calls=%async_computation.3 | async-start | bytes 8257536 | tf_op jit(solution)/shard_map/all_gather | solution.py:37
  12.9 58.6 %all-to-all-start.1 = ((bf16[128,8,512]{0,2,1:T(8,128)(2,1)}), bf16[128,8,512]{0,2,1:T(8,128)(2,1)S(1)}, u32[]{:S(2)}, u32[]{:S(2)}) async-start(bf16[128,8,512]{0,2,1:T(8,128)(2,1)} %bitcast.4), calls=%async_computation.1 | async-start | bytes 2097152 | tf_op jit(solution)/shard_map/all_to_all | solution.py:33
  71.5 22.3 %all-to-all-start = ((bf16[64,8,512]{2,0,1:T(8,128)(2,1)}), bf16[64,8,512]{2,0,1:T(8,128)(2,1)S(1)}, u32[]{:S(2)}, u32[]{:S(2)}) async-start(bf16[64,8,512]{2,0,1:T(8,128)(2,1)} %bitcast.29), calls=%async_computation | async-start | bytes 1048576 | tf_op jit(solution)/shard_map/all_to_all | solution.py:32
  208.9 10.1 %copy-start.3 = (f32[16]{0:T(128)}, f32[16]{0:T(128)S(1)}, u32[]{:S(2)}) copy-start(f32[16]{0:T(128)S(1)} %get-tuple-element.13) | copy-start | bytes 196
Sparse Core Ops, SparseCore 0:
  10.0 66.9 all-gather.2
  78.6 72.7 all-gather.4
where the time goes:
time: 232 us
  waiting for transfers between devices  123 us (53%)
  blocking collectives  45 us (19%)
  matrix products  20.5 us (9%)
  between operations  15.5 us (7%)
  local copies, waits for them, and re-layouts  12.8 us (6%)
  starting transfers between devices  9.9 us (4%)
  other arithmetic  4.81 us (2%)
    all_gather x1, waiting for transfers between devices, shards(): lax.all_gather(train_hidden, ('dp', 'sub'), axis=0, tiled=True)  57.7 us
    all_to_all x1, waiting for transfers between devices, shards(): lax.all_to_all(train_cotan, ('dp', 'sub'), split_axis=1, concat_axis=0, t...  51.4 us
    psum x1, blocking collectives, shards(): align = lax.psum(part_align, ('dp', 'tensor', 'sub'))  29.9 us
    psum x1, blocking collectives, shards(): val_total = lax.psum(count_local, ('dp', 'sub'))  15.1 us
    all_to_all x1, waiting for transfers between devices, shards(): lax.all_to_all(val_cotan, ('dp', 'sub'), split_axis=1, concat_axis=0, til...  13.4 us
    dot_general x1, matrix products, shards(): jnp.dot(train_every, val_grad, preferred_element_type=jnp.float32)  10.6 us
    dot_general x1, matrix products, shards(): lax.dot_general(train_every, weighted_cotan, contract_rows, preferred_ele...  8.79 us
    unnamed x10, local copies, waits for them, and re-layouts  8.21 us
  transfers between devices with their start and end apart: 4, of which 3 were waited for; matrix products, arithmetic and copies ran while one was open for 4% of the time, Pallas kernels for 0%

commit v1 on v0

v1 whole, which is shorter than its diff:
```python
import functools

import jax
import jax.numpy as jnp
from jax import lax
from jax.experimental import pallas as pl
from jax.experimental.pallas import tpu as pltpu
from jax.sharding import PartitionSpec as P

D = 4096
FF = 7168
LANES = 128
F32 = jnp.float32
BF16 = jnp.bfloat16
PIECES = 7


def membership(seq_len, seq_device, row_count, capacity):
    seq_order = jnp.arange(seq_len.shape[0], dtype=jnp.int32)
    shared = seq_device[:, None] == seq_device[None, :]
    earlier = seq_order[None, :] < seq_order[:, None]
    offset = jnp.sum(jnp.where(shared & earlier, seq_len[None, :], 0), axis=1)
    row_ids = jnp.arange(row_count, dtype=jnp.int32)
    holder = row_ids // capacity
    within = row_ids % capacity
    inside = (
        (seq_device[None, :] == holder[:, None])
        & (within[:, None] >= offset[None, :])
        & (within[:, None] < (offset + seq_len)[None, :])
    )
    return inside.astype(F32)


def kernel(
    nz, nx, hv_ref, cv_ref, count_ref, h_ref, c_ref, member_ref, len_ref,
    out_ref, weight_ref,
    h_all, hv_all, c_all, cv_all, grad, turned, weighted, acc, near, across, along,
    h_right, h_left, h_recv, h_give, h_get,
    hv_right, hv_left, hv_recv, hv_give, hv_get,
    c_send, c_recv, cv_send, cv_recv,
    near_send, near_recv, across_send, across_recv, along_send, along_recv,
):
    z = lax.axis_index("dp")
    x = lax.axis_index("tensor")
    s = lax.axis_index("sub")
    mate = 1 - s
    span = c_all.shape[3]
    toks, width = h_ref.shape
    vals = hv_ref.shape[0]

    barrier = pltpu.get_barrier_semaphore()
    for step in range(1, 2 * nz):
        other = lax.rem(z * 2 + s + step, 2 * nz)
        pl.semaphore_signal(barrier, inc=1, device_id={"dp": other // 2, "sub": lax.rem(other, 2)})
    for step in range(1, nx):
        pl.semaphore_signal(barrier, inc=1, device_id={"tensor": lax.rem(x + step, nx)})

    live = lax.broadcasted_iota(jnp.int32, hv_ref.shape, 0) < count_ref[0]
    hv_all[z, s] = jnp.where(live, hv_ref[...], jnp.zeros_like(hv_ref))
    h_all[z, s] = h_ref[...]
    pl.semaphore_wait(barrier, 2 * nz - 1 + nx - 1)

    def hop(full, b, k, rows, send, recv, target):
        ref = full.at[b, s, pl.ds(k * rows, rows)]
        return pltpu.make_async_remote_copy(
            src_ref=ref, dst_ref=ref, send_sem=send.at[b, k], recv_sem=recv.at[b, k],
            device_id=target,
        )

    class Line:
        def __init__(self, full, pieces, right, left, recv, give, get):
            self.full, self.pieces = full, pieces
            self.rows = full.shape[2] // pieces
            self.right_sem, self.left_sem, self.recv = right, left, recv
            self.give_sem, self.get = give, get

        def right(self, b, k):
            return hop(self.full, b, k, self.rows, self.right_sem, self.recv, {"dp": jnp.minimum(z + 1, nz - 1)})

        def left(self, b, k):
            return hop(self.full, b, k, self.rows, self.left_sem, self.recv, {"dp": jnp.maximum(z - 1, 0)})

        def give(self, b, k):
            return hop(self.full, b, k, self.rows, self.give_sem, self.get, {"sub": mate})

        def landed(self, b, k):
            self.right(b, k).wait_recv()

        def got(self, b):
            for k in range(self.pieces):
                self.give(b, k).wait_recv()

        def begin(self):
            for k in range(self.pieces):
                @pl.when(z < nz - 1)
                def _():
                    self.right(z, k).start()

                @pl.when(z > 0)
                def _():
                    self.left(z, k).start()

            for k in range(self.pieces):
                self.give(z, k).start()

        def relay(self, t):
            for k in range(self.pieces):
                @pl.when(z - t >= 0)
                def _():
                    b = z - t
                    self.landed(b, k)

                    @pl.when(z < nz - 1)
                    def _():
                        self.right(b, k).start()

                    self.give(b, k).start()

                @pl.when(z + t < nz)
                def _():
                    b = z + t
                    self.landed(b, k)

                    @pl.when(z > 0)
                    def _():
                        self.left(b, k).start()

                    self.give(b, k).start()

        def finish(self):
            def body(b, carry):
                for k in range(self.pieces):
                    self.give(b, k).wait_send()

                    @pl.when((b <= z) & (z < nz - 1))
                    def _():
                        self.right(b, k).wait_send()

                    @pl.when((b >= z) & (z > 0))
                    def _():
                        self.left(b, k).wait_send()

                return carry

            lax.fori_loop(0, nz, body, 0)

    hv_line = Line(hv_all, hv_right.shape[1], hv_right, hv_left, hv_recv, hv_give, hv_get)
    h_line = Line(h_all, h_right.shape[1], h_right, h_left, h_recv, h_give, h_get)

    def columns(src, full, send, recv, step):
        other = lax.rem(z * 2 + s + step, 2 * nz)
        return pltpu.make_async_remote_copy(
            src_ref=src.at[:, pl.ds(pl.multiple_of(other * span, span), span)],
            dst_ref=full.at[z, s],
            send_sem=send.at[step - 1], recv_sem=recv.at[step - 1],
            device_id={"dp": other // 2, "sub": lax.rem(other, 2)},
        )

    def each_column(do):
        def body(step, carry):
            do(step)
            return carry

        lax.fori_loop(1, 2 * nz, body, 0)

    def start_cv(step):
        columns(cv_ref, cv_all, cv_send, cv_recv, step).start()

    def start_c(step):
        columns(c_ref, c_all, c_send, c_recv, step).start()

    own = pl.ds(pl.multiple_of((z * 2 + s) * span, span), span)
    hv_line.begin()
    each_column(start_cv)
    h_line.begin()
    each_column(start_c)
    cv_all[z, s] = cv_ref[:, own]
    c_all[z, s] = c_ref[:, own]
    acc[...] = jnp.zeros_like(acc)

    def hv_step(t, carry):
        hv_line.relay(t)
        return carry

    lax.fori_loop(1, nz, hv_step, 0)
    each_column(lambda step: columns(cv_ref, cv_all, cv_send, cv_recv, step).wait())

    def hv_mate(b, carry):
        hv_line.got(b)
        return carry

    lax.fori_loop(0, nz, hv_mate, 0)

    piece = width // PIECES
    cv_flat = cv_all[...].reshape(2 * nz * vals, span)

    def grad_piece(i, carry):
        at = pl.ds(pl.multiple_of(i * piece, LANES), piece)
        left = hv_all[:, :, :, at].reshape(2 * nz * vals, piece)
        grad[at, :] = lax.dot_general(
            left, cv_flat, (((0,), (0,)), ((), ())), preferred_element_type=F32
        ).astype(BF16)
        return carry

    lax.fori_loop(0, PIECES, grad_piece, 0)
    each_column(lambda step: columns(c_ref, c_all, c_send, c_recv, step).wait())

    def use(b, core):
        block = h_all[b, core]
        projected = jnp.dot(block, grad[...], preferred_element_type=F32)
        token = jnp.sum(projected * c_all[b, core].astype(F32), axis=1, keepdims=True)
        acc[0:1, :] += jnp.sum(token * member_ref[b, core], axis=0, keepdims=True)
        spot = pl.ds(pl.multiple_of((b * 2 + core) * toks, LANES), toks)

        def turn(i, carry):
            at = pl.ds(pl.multiple_of(i * piece, LANES), piece)
            turned[at, spot] = h_all[b, core, :, at].T
            return carry

        lax.fori_loop(0, PIECES, turn, 0)

    use(z, s)
    h_line.got(z)
    use(z, mate)

    def both(b):
        use(b, s)
        h_line.got(b)
        use(b, mate)

    def h_step(t, carry):
        h_line.relay(t)

        @pl.when(z - t >= 0)
        def _():
            both(z - t)

        @pl.when(z + t < nz)
        def _():
            both(z + t)

        return carry

    lax.fori_loop(1, nz, h_step, 0)

    row = lax.broadcasted_iota(jnp.int32, acc.shape, 0)
    counted = jnp.where(row == 1, count_ref[0].astype(F32), acc[...])

    def exchange(value, buf, here, n, axis, send, recv):
        buf[here] = value
        copies = []
        for step in range(1, n):
            copy = pltpu.make_async_remote_copy(
                src_ref=buf.at[here], dst_ref=buf.at[here],
                send_sem=send.at[step - 1], recv_sem=recv.at[step - 1],
                device_id={axis: lax.rem(here + step, n)},
            )
            copy.start()
            copies.append(copy)
        for copy in copies:
            copy.wait()
        total = buf[0]
        for i in range(1, n):
            total = total + buf[i]
        return total

    total = exchange(counted, near, s, 2, "sub", near_send, near_recv)
    if nx > 1:
        total = exchange(total, across, x, nx, "tensor", across_send, across_recv)
    total = exchange(total, along, z, nz, "dp", along_send, along_recv)
    align = total[0:1, :]
    val_total = total[1:2, :] / float(nx)
    lengths = len_ref[...]
    score = align / jnp.sqrt(val_total * jnp.maximum(lengths, 1.0) * float(FF) * float(D))
    weight = 1.0 / (1.0 + jnp.exp(-score))
    weight_ref[...] = weight
    mass = jnp.sum(weight * lengths, axis=1, keepdims=True)
    root = jnp.sqrt(mass)

    def weigh(b, carry):
        for core in range(2):
            each = jnp.sum(member_ref[b, core] * weight, axis=1, keepdims=True)
            spot = pl.ds(pl.multiple_of((b * 2 + core) * toks, LANES), toks)
            weighted[spot, :] = (each * c_all[b, core].astype(F32)).astype(BF16)
        return carry

    lax.fori_loop(0, nz, weigh, 0)

    def final(i, carry):
        at = pl.ds(pl.multiple_of(i * piece, LANES), piece)
        product = jnp.dot(turned[at, :], weighted[...], preferred_element_type=F32)
        out_ref[at, :] = (product / root).astype(BF16)
        return carry

    lax.fori_loop(0, PIECES, final, 0)
    hv_line.finish()
    h_line.finish()


def shards(nz, nx, val_hidden, val_cotan, val_count, train_hidden, train_cotan, seq_len, seq_device):
    vals, width = val_hidden.shape
    toks = train_hidden.shape[0]
    span = D // (2 * nz)
    seqs = seq_len.shape[0]
    member = membership(seq_len, seq_device, 2 * nz * toks, toks)
    member = jnp.pad(member, ((0, 0), (0, LANES - seqs))).reshape(nz, 2, toks, LANES)
    lengths = jnp.pad(seq_len.astype(F32), (0, LANES - seqs)).reshape(1, LANES)
    sem = lambda *shape: pltpu.SemaphoreType.DMA(shape)
    hp, vp = (4, 2) if nz <= 4 else (1, 1)
    vmem = pl.BlockSpec(memory_space=pltpu.VMEM)
    smem = pl.BlockSpec(memory_space=pltpu.SMEM)
    out, weight = pl.pallas_call(
        functools.partial(kernel, nz, nx),
        out_shape=(
            jax.ShapeDtypeStruct((width, span), BF16),
            jax.ShapeDtypeStruct((1, LANES), F32),
        ),
        in_specs=[vmem, vmem, smem, vmem, vmem, vmem, vmem],
        out_specs=(vmem, vmem),
        scratch_shapes=[
            pltpu.VMEM((nz, 2, toks, width), BF16),
            pltpu.VMEM((nz, 2, vals, width), BF16),
            pltpu.VMEM((nz, 2, toks, span), BF16),
            pltpu.VMEM((nz, 2, vals, span), BF16),
            pltpu.VMEM((width, span), BF16),
            pltpu.VMEM((width, 2 * nz * toks), BF16),
            pltpu.VMEM((2 * nz * toks, span), BF16),
            pltpu.VMEM((8, LANES), F32),
            pltpu.VMEM((2, 8, LANES), F32),
            pltpu.VMEM((nx, 8, LANES), F32),
            pltpu.VMEM((nz, 8, LANES), F32),
            sem(nz, hp), sem(nz, hp), sem(nz, hp), sem(nz, hp), sem(nz, hp),
            sem(nz, vp), sem(nz, vp), sem(nz, vp), sem(nz, vp), sem(nz, vp),
            sem(2 * nz - 1), sem(2 * nz - 1), sem(2 * nz - 1), sem(2 * nz - 1),
            sem(1), sem(1), sem(max(nx - 1, 1)), sem(max(nx - 1, 1)), sem(nz - 1), sem(nz - 1),
        ],
        compiler_params=pltpu.CompilerParams(
            collective_id=0, has_side_effects=True, vmem_limit_bytes=56 * 1024 * 1024
        ),
        cost_estimate=pl.CostEstimate(flops=9400000000, bytes_accessed=20000000, transcendentals=0),
    )(val_hidden, val_cotan, val_count, train_hidden, train_cotan, member, lengths)
    return out, weight[0, :seqs]


def solution(mesh):
    return jax.shard_map(
        functools.partial(shards, mesh.shape["dp"], mesh.shape["tensor"]),
        mesh=mesh,
        in_specs=(
            P(("groups", "dp", "sub"), "tensor"),
            P(("groups", "dp", "sub"), None),
            P(("groups", "dp", "sub")),
            P(("groups", "dp", "sub"), "tensor"),
            P(("groups", "dp", "sub"), None),
            P("groups"),
            P("groups"),
        ),
        out_specs=(P(("groups", "tensor"), ("dp", "sub")), P("groups")),
        check_vma=False,
    )
```

time: 232 us -> 160 us (0.69)
  Pallas kernels: 0 us -> 149 us
  waiting for transfers between devices: 123 us -> 0 us
  blocking collectives: 45 us -> 0 us
  matrix products: 20.5 us -> 0 us
  between operations: 15.5 us -> 1.3 us
  starting transfers between devices: 9.9 us -> 0 us
  local copies, waits for them, and re-layouts: 12.8 us -> 6.81 us
  other arithmetic: 4.81 us -> 2.43 us
    pallas_call x0 -> x1, Pallas kernels: none -> 149 us  [shards(): pl.pallas_call(functools.partial(kernel, nz, nx), out_shape=(jax.ShapeDty...]
    all_to_all x2 -> x0, waiting for transfers between devices: 64.8 us -> none  [the longest x1 51.4 us: shards(): lax.all_to_all(train_cotan, ('dp', 'sub'), split_axis=1, concat_axis=0, t...]
    all_gather x2 -> x0, waiting for transfers between devices: 57.7 us -> none  [the longest x1 57.7 us: shards(): lax.all_gather(train_hidden, ('dp', 'sub'), axis=0, tiled=True)]
    psum x2 -> x0, blocking collectives: 45 us -> none  [the longest x1 29.9 us: shards(): align = lax.psum(part_align, ('dp', 'tensor', 'sub'))]
    dot_general x4 -> x0, matrix products: 20.5 us -> none  [the longest x1 10.6 us: shards(): jnp.dot(train_every, val_grad, preferred_element_type=jnp.float32)]
    all_to_all x2 -> x0, starting transfers between devices: 9.83 us -> none  [the longest x1 6.33 us: shards(): lax.all_to_all(train_cotan, ('dp', 'sub'), split_axis=1, concat_axis=0, t...]
    unnamed x10 -> x1, local copies, waits for them, and re-layouts: 8.21 us -> 4.11 us
    convert_element_type x2 -> x0, local copies, waits for them, and re-layouts: 3.73 us -> none  [shards(): token_part = jnp.sum(projected * train_columns, axis=1)]
  transfers between devices with their start and end apart: 4 -> 0, of which waited for: 3 -> 0; matrix products, arithmetic and copies ran while one was open for 4% -> 0% of each run, Pallas kernels for 0% -> 0%
where the time goes in v1:
time: 160 us
  Pallas kernels  149 us (93%)
  local copies, waits for them, and re-layouts  6.81 us (4%)
  other arithmetic  2.43 us (2%)
    pallas_call x1, Pallas kernels, shards(): pl.pallas_call(functools.partial(kernel, nz, nx), out_shape=(jax.ShapeDty...  149 us
    unnamed x1, local copies, waits for them, and re-layouts  4.11 us

profile of v1, /device:TPU:0, one launch (start us, length us, event | category | flops | bytes accessed | tf_op | source)
XLA Modules:
  0.0 159.8 jit_solution(16596077211474454351)
XLA Ops:
  1.3 0.9 select_reduce_fusion
  2.2 0.7 fusion.8
  2.9 0.5 pad_bitcast_fusion.len_ref
  3.4 0.7 compare_and_fusion
  4.2 1.0 copy.9
  5.2 149.3 %shard_map.86 = (bf16[3584,512]{1,0:T(8,128)(2,1)}, f32[1,128]{1,0:T(1,128)}) custom-call(bf16[64,3584]{1,0:T(8,128)(2,1)} %hv_ref.1, bf16[64,4096]{1,0:T(8,128)(2,1)} %cv_ref.1, s32[1]{0:T(128)S(6)} %copy.11.count_ref, bf16[128,3584]{1,0:T(8,128)(2,1)} %h_ref.1, bf16[128,4096]{1,0:T(8,128)(2,1)} %c_ref.1, f32[4,2,128,128]{3,2,1,0:T(8,128)} %bitcast.5, ...), custom_call_target="tpu_custom_call" | custom-call | flops 9400000512 | bytes 20000000 | tf_op jit(solution)/shard_map/pallas_call | solution.py:312
  154.5 1.2 slice_bitcast_fusion
  155.7 4.1 %copy.12 = bf16[3584,512]{1,0:T(8,128)(2,1)} copy(bf16[3584,512]{1,0:T(8,128)(2,1)} %get-tuple-element.12) | data formatting | bytes 7340032
  (2 shorter events, 0.0 us)

commit v2 on v1

--- a/solution.py
+++ b/solution.py
@@ -15,29 +15,13 @@
 PIECES = 7
 
 
-def membership(seq_len, seq_device, row_count, capacity):
-    seq_order = jnp.arange(seq_len.shape[0], dtype=jnp.int32)
-    shared = seq_device[:, None] == seq_device[None, :]
-    earlier = seq_order[None, :] < seq_order[:, None]
-    offset = jnp.sum(jnp.where(shared & earlier, seq_len[None, :], 0), axis=1)
-    row_ids = jnp.arange(row_count, dtype=jnp.int32)
-    holder = row_ids // capacity
-    within = row_ids % capacity
-    inside = (
-        (seq_device[None, :] == holder[:, None])
-        & (within[:, None] >= offset[None, :])
-        & (within[:, None] < (offset + seq_len)[None, :])
-    )
-    return inside.astype(F32)
-
-
 def kernel(
-    nz, nx, hv_ref, cv_ref, count_ref, h_ref, c_ref, member_ref, len_ref,
+    nz, nx, hv_ref, cv_ref, count_ref, h_ref, c_ref, len_ref, dev_ref,
     out_ref, weight_ref,
-    h_all, hv_all, c_all, cv_all, grad, turned, weighted, acc, near, across, along,
+    h_all, cv_all, c_all, kept, turned, weighted, k1_all, k2_out, k2_all, near, across, along,
     h_right, h_left, h_recv, h_give, h_get,
-    hv_right, hv_left, hv_recv, hv_give, hv_get,
-    c_send, c_recv, cv_send, cv_recv,
+    cv_right, cv_left, cv_recv, cv_give, cv_get,
+    c_send, c_recv, c_swap, c_swapped, k2_send, k2_recv, k2_swap, k2_swapped,
     near_send, near_recv, across_send, across_recv, along_send, along_recv,
 ):
     z = lax.axis_index("dp")
@@ -47,6 +31,10 @@
     span = c_all.shape[3]
     toks, width = h_ref.shape
     vals = hv_ref.shape[0]
+    planes, _, _, rows_v, _ = k2_all.shape
+    plane = x if planes > 1 else 0
+    rows_c = toks // nx
+    seqs = len_ref.shape[0]
 
     barrier = pltpu.get_barrier_semaphore()
     for step in range(1, 2 * nz):
@@ -55,8 +43,7 @@
     for step in range(1, nx):
         pl.semaphore_signal(barrier, inc=1, device_id={"tensor": lax.rem(x + step, nx)})
 
-    live = lax.broadcasted_iota(jnp.int32, hv_ref.shape, 0) < count_ref[0]
-    hv_all[z, s] = jnp.where(live, hv_ref[...], jnp.zeros_like(hv_ref))
+    cv_all[z, s] = cv_ref[pl.ds(pl.multiple_of(plane * rows_v, 16), rows_v), :]
     h_all[z, s] = h_ref[...]
     pl.semaphore_wait(barrier, 2 * nz - 1 + nx - 1)
 
@@ -144,72 +131,99 @@
 
             lax.fori_loop(0, nz, body, 0)
 
-    hv_line = Line(hv_all, hv_right.shape[1], hv_right, hv_left, hv_recv, hv_give, hv_get)
+    cv_line = Line(cv_all, cv_right.shape[1], cv_right, cv_left, cv_recv, cv_give, cv_get)
     h_line = Line(h_all, h_right.shape[1], h_right, h_left, h_recv, h_give, h_get)
 
-    def columns(src, full, send, recv, step):
-        other = lax.rem(z * 2 + s + step, 2 * nz)
+    def others(do):
+        def body(step, carry):
+            other = lax.rem(z * 2 + s + step, 2 * nz)
+            do(step, other // 2, lax.rem(other, 2))
+            return carry
+
+        lax.fori_loop(1, 2 * nz, body, 0)
+
+    part = pl.ds(pl.multiple_of(x * rows_c, 16), rows_c)
+
+    def columns(step, b, core):
         return pltpu.make_async_remote_copy(
-            src_ref=src.at[:, pl.ds(pl.multiple_of(other * span, span), span)],
-            dst_ref=full.at[z, s],
-            send_sem=send.at[step - 1], recv_sem=recv.at[step - 1],
-            device_id={"dp": other // 2, "sub": lax.rem(other, 2)},
+            src_ref=c_ref.at[part, pl.ds(pl.multiple_of((b * 2 + core) * span, span), span)],
+            dst_ref=c_all.at[z, s, part],
+            send_sem=c_send.at[step - 1], recv_sem=c_recv.at[step - 1],
+            device_id={"dp": b, "sub": core},
         )
 
-    def each_column(do):
-        def body(step, carry):
-            do(step)
-            return carry
-
-        lax.fori_loop(1, 2 * nz, body, 0)
-
-    def start_cv(step):
-        columns(cv_ref, cv_all, cv_send, cv_recv, step).start()
-
-    def start_c(step):
-        columns(c_ref, c_all, c_send, c_recv, step).start()
-
+    def products(step, b, core):
+        return pltpu.make_async_remote_copy(
+            src_ref=k2_out.at[b, core], dst_ref=k2_all.at[plane, z, s],
+            send_sem=k2_send.at[step - 1], recv_sem=k2_recv.at[step - 1],
+            device_id={"dp": b, "sub": core},
+        )
+
+    def swaps():
+        copies = []
+        for step in range(1, nx):
+            peer = {"tensor": lax.rem(x + step, nx)}
+            copies.append(pltpu.make_async_remote_copy(
+                src_ref=c_all.at[:, :, part], dst_ref=c_all.at[:, :, part],
+                send_sem=c_swap.at[step - 1], recv_sem=c_swapped.at[step - 1], device_id=peer,
+            ))
+            if planes > 1:
+                copies.append(pltpu.make_async_remote_copy(
+                    src_ref=k2_all.at[plane], dst_ref=k2_all.at[plane],
+                    send_sem=k2_swap.at[step - 1], recv_sem=k2_swapped.at[step - 1], device_id=peer,
+                ))
+        return copies
+
+    cv_line.begin()
+    h_line.begin()
+    others(lambda *at: columns(*at).start())
     own = pl.ds(pl.multiple_of((z * 2 + s) * span, span), span)
-    hv_line.begin()
-    each_column(start_cv)
-    h_line.begin()
-    each_column(start_c)
-    cv_all[z, s] = cv_ref[:, own]
-    c_all[z, s] = c_ref[:, own]
-    acc[...] = jnp.zeros_like(acc)
-
-    def hv_step(t, carry):
-        hv_line.relay(t)
-        return carry
-
-    lax.fori_loop(1, nz, hv_step, 0)
-    each_column(lambda step: columns(cv_ref, cv_all, cv_send, cv_recv, step).wait())
-
-    def hv_mate(b, carry):
-        hv_line.got(b)
-        return carry
-
-    lax.fori_loop(0, nz, hv_mate, 0)
+    c_all[z, s, part] = c_ref[part, own]
+    live = lax.broadcasted_iota(jnp.int32, hv_ref.shape, 0) < count_ref[0]
+    kept[...] = jnp.where(live, hv_ref[...], jnp.zeros_like(hv_ref))
+
+    lane = lax.broadcasted_iota(jnp.int32, (1, LANES), 1)
+
+    def lay(j, rows):
+        lens, devs = rows
+        return jnp.where(lane == j, len_ref[j], lens), jnp.where(lane == j, dev_ref[j], devs)
+
+    lens, devs = lax.fori_loop(0, seqs, lay, (jnp.zeros_like(lane), jnp.full_like(lane, -1)))
+
+    def place(j, offset):
+        return offset + jnp.where((devs == dev_ref[j]) & (lane > j), len_ref[j], 0)
+
+    offset = lax.fori_loop(0, seqs, place, jnp.zeros_like(lane))
+
+    def member(b, core):
+        within = lax.broadcasted_iota(jnp.int32, (toks, LANES), 0)
+        inside = (devs == b * 2 + core) & (within >= offset) & (within < offset + lens)
+        return inside.astype(F32)
+
+    def cv_step(t, carry):
+        cv_line.relay(t)
+        return carry
+
+    lax.fori_loop(1, nz, cv_step, 0)
+
+    def multiply(b, carry):
+        cv_line.got(b)
+        for core in range(2):
+            k2_out[b, core] = lax.dot_general(
+                cv_all[b, core], c_ref[...], (((1,), (1,)), ((), ())), preferred_element_type=F32
+            )
+        return carry
+
+    lax.fori_loop(0, nz, multiply, 0)
+    others(lambda *at: products(*at).start())
+    k2_all[plane, z, s] = k2_out[z, s]
 
     piece = width // PIECES
-    cv_flat = cv_all[...].reshape(2 * nz * vals, span)
-
-    def grad_piece(i, carry):
-        at = pl.ds(pl.multiple_of(i * piece, LANES), piece)
-        left = hv_all[:, :, :, at].reshape(2 * nz * vals, piece)
-        grad[at, :] = lax.dot_general(
-            left, cv_flat, (((0,), (0,)), ((), ())), preferred_element_type=F32
-        ).astype(BF16)
-        return carry
-
-    lax.fori_loop(0, PIECES, grad_piece, 0)
-    each_column(lambda step: columns(c_ref, c_all, c_send, c_recv, step).wait())
 
     def use(b, core):
-        block = h_all[b, core]
-        projected = jnp.dot(block, grad[...], preferred_element_type=F32)
-        token = jnp.sum(projected * c_all[b, core].astype(F32), axis=1, keepdims=True)
-        acc[0:1, :] += jnp.sum(token * member_ref[b, core], axis=0, keepdims=True)
+        k1_all[b, core] = lax.dot_general(
+            kept[...], h_all[b, core], (((1,), (1,)), ((), ())), preferred_element_type=F32
+        )
         spot = pl.ds(pl.multiple_of((b * 2 + core) * toks, LANES), toks)
 
         def turn(i, carry):
@@ -229,6 +243,13 @@
         use(b, mate)
 
     def h_step(t, carry):
+        @pl.when(t == nz - 1)
+        def _():
+            others(lambda *at: products(*at).wait())
+            others(lambda *at: columns(*at).wait())
+            for copy in swaps():
+                copy.start()
+
         h_line.relay(t)
 
         @pl.when(z - t >= 0)
@@ -242,9 +263,23 @@
         return carry
 
     lax.fori_loop(1, nz, h_step, 0)
-
-    row = lax.broadcasted_iota(jnp.int32, acc.shape, 0)
-    counted = jnp.where(row == 1, count_ref[0].astype(F32), acc[...])
+    for copy in swaps():
+        copy.wait()
+
+    def align_block(b, total):
+        for core in range(2):
+            product = jnp.zeros((8, toks), F32)
+            for i in range(planes):
+                both_k = k1_all[b, core, i * rows_v : (i + 1) * rows_v] * k2_all[i, b, core]
+                product = product + jnp.sum(both_k.reshape(rows_v // 8, 8, toks), axis=0)
+            token = jnp.sum(product.T, axis=1, keepdims=True)
+            total = total + jnp.sum(token * member(b, core), axis=0, keepdims=True)
+        return total
+
+    acc = lax.fori_loop(0, nz, align_block, jnp.zeros((1, LANES), F32))
+
+    row = lax.broadcasted_iota(jnp.int32, (8, LANES), 0)
+    counted = jnp.where(row == 1, count_ref[0].astype(F32), acc)
 
     def exchange(value, buf, here, n, axis, send, recv):
         buf[here] = value
@@ -270,16 +305,16 @@
     total = exchange(total, along, z, nz, "dp", along_send, along_recv)
     align = total[0:1, :]
     val_total = total[1:2, :] / float(nx)
-    lengths = len_ref[...]
+    lengths = lens.astype(F32)
     score = align / jnp.sqrt(val_total * jnp.maximum(lengths, 1.0) * float(FF) * float(D))
     weight = 1.0 / (1.0 + jnp.exp(-score))
-    weight_ref[...] = weight
+    weight_ref[...] = weight[:, :seqs]
     mass = jnp.sum(weight * lengths, axis=1, keepdims=True)
     root = jnp.sqrt(mass)
 
     def weigh(b, carry):
         for core in range(2):
-            each = jnp.sum(member_ref[b, core] * weight, axis=1, keepdims=True)
+            each = jnp.sum(member(b, core) * weight, axis=1, keepdims=True)
             spot = pl.ds(pl.multiple_of((b * 2 + core) * toks, LANES), toks)
             weighted[spot, :] = (each * c_all[b, core].astype(F32)).astype(BF16)
         return carry
@@ -293,7 +328,7 @@
         return carry
 
     lax.fori_loop(0, PIECES, final, 0)
-    hv_line.finish()
+    cv_line.finish()
     h_line.finish()
 
 
@@ -302,9 +337,8 @@
     toks = train_hidden.shape[0]
     span = D // (2 * nz)
     seqs = seq_len.shape[0]
-    member = membership(seq_len, seq_device, 2 * nz * toks, toks)
-    member = jnp.pad(member, ((0, 0), (0, LANES - seqs))).reshape(nz, 2, toks, LANES)
-    lengths = jnp.pad(seq_len.astype(F32), (0, LANES - seqs)).reshape(1, LANES)
+    planes = nx if vals % (16 * nx) == 0 else 1
+    rows_v = vals // planes
     sem = lambda *shape: pltpu.SemaphoreType.DMA(shape)
     hp, vp = (4, 2) if nz <= 4 else (1, 1)
     vmem = pl.BlockSpec(memory_space=pltpu.VMEM)
@@ -313,33 +347,35 @@
         functools.partial(kernel, nz, nx),
         out_shape=(
             jax.ShapeDtypeStruct((width, span), BF16),
-            jax.ShapeDtypeStruct((1, LANES), F32),
+            jax.ShapeDtypeStruct((1, seqs), F32),
         ),
-        in_specs=[vmem, vmem, smem, vmem, vmem, vmem, vmem],
+        in_specs=[vmem, vmem, smem, vmem, vmem, smem, smem],
         out_specs=(vmem, vmem),
         scratch_shapes=[
             pltpu.VMEM((nz, 2, toks, width), BF16),
-            pltpu.VMEM((nz, 2, vals, width), BF16),
+            pltpu.VMEM((nz, 2, rows_v, D), BF16),
             pltpu.VMEM((nz, 2, toks, span), BF16),
-            pltpu.VMEM((nz, 2, vals, span), BF16),
-            pltpu.VMEM((width, span), BF16),
+            pltpu.VMEM((vals, width), BF16),
             pltpu.VMEM((width, 2 * nz * toks), BF16),
             pltpu.VMEM((2 * nz * toks, span), BF16),
-            pltpu.VMEM((8, LANES), F32),
+            pltpu.VMEM((nz, 2, vals, toks), F32),
+            pltpu.VMEM((nz, 2, rows_v, toks), F32),
+            pltpu.VMEM((planes, nz, 2, rows_v, toks), F32),
             pltpu.VMEM((2, 8, LANES), F32),
             pltpu.VMEM((nx, 8, LANES), F32),
             pltpu.VMEM((nz, 8, LANES), F32),
             sem(nz, hp), sem(nz, hp), sem(nz, hp), sem(nz, hp), sem(nz, hp),
             sem(nz, vp), sem(nz, vp), sem(nz, vp), sem(nz, vp), sem(nz, vp),
-            sem(2 * nz - 1), sem(2 * nz - 1), sem(2 * nz - 1), sem(2 * nz - 1),
+            sem(2 * nz - 1), sem(2 * nz - 1), sem(max(nx - 1, 1)), sem(max(nx - 1, 1)),
+            sem(2 * nz - 1), sem(2 * nz - 1), sem(max(nx - 1, 1)), sem(max(nx - 1, 1)),
             sem(1), sem(1), sem(max(nx - 1, 1)), sem(max(nx - 1, 1)), sem(nz - 1), sem(nz - 1),
         ],
         compiler_params=pltpu.CompilerParams(
             collective_id=0, has_side_effects=True, vmem_limit_bytes=56 * 1024 * 1024
         ),
-        cost_estimate=pl.CostEstimate(flops=9400000000, bytes_accessed=20000000, transcendentals=0),
-    )(val_hidden, val_cotan, val_count, train_hidden, train_cotan, member, lengths)
-    return out, weight[0, :seqs]
+        cost_estimate=pl.CostEstimate(flops=4500000000, bytes_accessed=20000000, transcendentals=0),
+    )(val_hidden, val_cotan, val_count, train_hidden, train_cotan, seq_len, seq_device)
+    return out, weight.reshape(seqs)
 
 
 def solution(mesh):

time: 160 us -> 125 us (0.78)
  Pallas kernels: 149 us -> 119 us
  other arithmetic: 2.43 us -> 0 us
  local copies, waits for them, and re-layouts: 6.81 us -> 4.63 us
    pallas_call x1, Pallas kernels: 149 us -> 119 us  [shards(): pl.pallas_call(functools.partial(kernel, nz, nx), out_shape=(jax.ShapeDty...]
    unnamed x1 -> x4, local copies, waits for them, and re-layouts: 4.11 us -> 4.63 us
where the time goes in v2:
time: 125 us
  Pallas kernels  119 us (95%)
  local copies, waits for them, and re-layouts  4.63 us (4%)
  between operations  1.29 us (1%)
    pallas_call x1, Pallas kernels, shards(): pl.pallas_call(functools.partial(kernel, nz, nx), out_shape=(jax.ShapeDty...  119 us
    unnamed x4, local copies, waits for them, and re-layouts  4.63 us

profile of v2, /device:TPU:0, one launch (start us, length us, event | category | flops | bytes accessed | tf_op | source)
XLA Modules:
  0.0 124.8 jit_solution(10890172198708157976)
XLA Ops:
  1.3 118.9 %shard_map.86 = (bf16[3584,512]{1,0:T(8,128)(2,1)}, f32[1,16]{1,0:T(1,128)}) custom-call(bf16[64,3584]{1,0:T(8,128)(2,1)} %hv_ref.1, bf16[64,4096]{1,0:T(8,128)(2,1)} %cv_ref.1, s32[1]{0:T(128)S(6)} %copy.11.count_ref, bf16[128,3584]{1,0:T(8,128)(2,1)} %h_ref.1, bf16[128,4096]{1,0:T(8,128)(2,1)} %c_ref.1, s32[16]{0:T(128)} %len_ref.1, s32[16]{0:T(128)} %dev_ref.1), custom_call_target="tpu_custom_call" | custom-call | flops 4499999744 | bytes 20000000 | tf_op jit(solution)/shard_map/pallas_call | solution.py:346
  120.2 0.0 copy-start
  120.2 4.1 %copy.12 = bf16[3584,512]{1,0:T(8,128)(2,1)} copy(bf16[3584,512]{1,0:T(8,128)(2,1)} %get-tuple-element.8) | data formatting | bytes 7340032
  124.3 0.0 copy-done
  124.3 0.5 copy.13
Async XLA Ops:
  120.2 4.1 %copy-start = (f32[1,16]{1,0:T(1,128)S(1)}, f32[1,16]{1,0:T(1,128)}, u32[]{:S(2)}) copy-start(f32[1,16]{1,0:T(1,128)} %get-tuple-element.5) | copy-start | bytes 196

commit v3 on v2

--- a/solution.py
+++ b/solution.py
@@ -18,10 +18,10 @@
 def kernel(
     nz, nx, hv_ref, cv_ref, count_ref, h_ref, c_ref, len_ref, dev_ref,
     out_ref, weight_ref,
-    h_all, cv_all, c_all, kept, turned, weighted, k1_all, k2_out, k2_all, near, across, along,
+    h_all, cv_all, c_all, kept, turned, weighted, k1_all, c_far, k2_out, k2_all, near, across, along,
     h_right, h_left, h_recv, h_give, h_get,
     cv_right, cv_left, cv_recv, cv_give, cv_get,
-    c_send, c_recv, c_swap, c_swapped, k2_send, k2_recv, k2_swap, k2_swapped,
+    c_send, c_recv, c_swap, c_swapped, k2_send, k2_recv, k2_swap, k2_swapped, far_send, far_recv, far_swap, far_swapped,
     near_send, near_recv, across_send, across_recv, along_send, along_recv,
 ):
     z = lax.axis_index("dp")
@@ -54,8 +54,15 @@
             device_id=target,
         )
 
+    inner = (z > 0) & (z < nz - 1)
+    beside = (z == 1) | (z == nz - 2)
+    end = jnp.where(z == 1, 0, nz - 1)
+
     class Line:
-        def __init__(self, full, pieces, right, left, recv, give, get):
+        def __init__(self, skip, full, pieces, right, left, recv, give, get):
+            self.sharing = inner if skip else (z >= 0)
+            self.sends_right = z < nz - (2 if skip else 1)
+            self.sends_left = z > (1 if skip else 0)
             self.full, self.pieces = full, pieces
             self.rows = full.shape[2] // pieces
             self.right_sem, self.left_sem, self.recv = right, left, recv
@@ -79,36 +86,38 @@
 
         def begin(self):
             for k in range(self.pieces):
-                @pl.when(z < nz - 1)
+                @pl.when(self.sends_right)
                 def _():
                     self.right(z, k).start()
 
-                @pl.when(z > 0)
+                @pl.when(self.sends_left)
                 def _():
                     self.left(z, k).start()
 
             for k in range(self.pieces):
-                self.give(z, k).start()
+                @pl.when(self.sharing)
+                def _():
+                    self.give(z, k).start()
 
         def relay(self, t):
             for k in range(self.pieces):
-                @pl.when(z - t >= 0)
+                @pl.when((z - t >= 0) & self.sharing)
                 def _():
                     b = z - t
                     self.landed(b, k)
 
-                    @pl.when(z < nz - 1)
+                    @pl.when(self.sends_right)
                     def _():
                         self.right(b, k).start()
 
                     self.give(b, k).start()
 
-                @pl.when(z + t < nz)
+                @pl.when((z + t < nz) & self.sharing)
                 def _():
                     b = z + t
                     self.landed(b, k)
 
-                    @pl.when(z > 0)
+                    @pl.when(self.sends_left)
                     def _():
                         self.left(b, k).start()
 
@@ -117,13 +126,15 @@
         def finish(self):
             def body(b, carry):
                 for k in range(self.pieces):
-                    self.give(b, k).wait_send()
-
-                    @pl.when((b <= z) & (z < nz - 1))
+                    @pl.when(self.sharing)
+                    def _():
+                        self.give(b, k).wait_send()
+
+                    @pl.when((b <= z) & self.sends_right & (self.sharing | (b == z)))
                     def _():
                         self.right(b, k).wait_send()
 
-                    @pl.when((b >= z) & (z > 0))
+                    @pl.when((b >= z) & self.sends_left & (self.sharing | (b == z)))
                     def _():
                         self.left(b, k).wait_send()
 
@@ -131,8 +142,8 @@
 
             lax.fori_loop(0, nz, body, 0)
 
-    cv_line = Line(cv_all, cv_right.shape[1], cv_right, cv_left, cv_recv, cv_give, cv_get)
-    h_line = Line(h_all, h_right.shape[1], h_right, h_left, h_recv, h_give, h_get)
+    cv_line = Line(True, cv_all, cv_right.shape[1], cv_right, cv_left, cv_recv, cv_give, cv_get)
+    h_line = Line(False, h_all, h_right.shape[1], h_right, h_left, h_recv, h_give, h_get)
 
     def others(do):
         def body(step, carry):
@@ -152,12 +163,35 @@
             device_id={"dp": b, "sub": core},
         )
 
-    def products(step, b, core):
+    def products(which, step, b, core):
         return pltpu.make_async_remote_copy(
-            src_ref=k2_out.at[b, core], dst_ref=k2_all.at[plane, z, s],
-            send_sem=k2_send.at[step - 1], recv_sem=k2_recv.at[step - 1],
+            src_ref=k2_out.at[which, b, core], dst_ref=k2_all.at[plane, (z, end)[which], s],
+            send_sem=k2_send.at[which, step - 1], recv_sem=k2_recv.at[(z, end)[which], s],
             device_id={"dp": b, "sub": core},
         )
+
+    def product_landed(step, b, core):
+        ref = k2_all.at[plane, b, core]
+        pltpu.make_async_remote_copy(
+            src_ref=ref, dst_ref=ref, send_sem=k2_send.at[0, 0], recv_sem=k2_recv.at[b, core],
+            device_id={"sub": mate},
+        ).wait_recv()
+
+    def far():
+        return pltpu.make_async_remote_copy(
+            src_ref=c_ref.at[part], dst_ref=c_far.at[part], send_sem=far_send.at[0], recv_sem=far_recv.at[0],
+            device_id={"dp": jnp.where(z == 0, 1, jnp.where(z == nz - 1, nz - 2, end))},
+        )
+
+    def far_swaps():
+        return [
+            pltpu.make_async_remote_copy(
+                src_ref=c_far.at[part], dst_ref=c_far.at[part],
+                send_sem=far_swap.at[step - 1], recv_sem=far_swapped.at[step - 1],
+                device_id={"tensor": lax.rem(x + step, nx)},
+            )
+            for step in range(1, nx)
+        ]
 
     def swaps():
         copies = []
@@ -174,6 +208,10 @@
                 ))
         return copies
 
+    @pl.when(jnp.logical_not(inner))
+    def _():
+        far().start()
+
     cv_line.begin()
     h_line.begin()
     others(lambda *at: columns(*at).start())
@@ -200,23 +238,17 @@
         inside = (devs == b * 2 + core) & (within >= offset) & (within < offset + lens)
         return inside.astype(F32)
 
-    def cv_step(t, carry):
-        cv_line.relay(t)
-        return carry
-
-    lax.fori_loop(1, nz, cv_step, 0)
-
-    def multiply(b, carry):
-        cv_line.got(b)
-        for core in range(2):
-            k2_out[b, core] = lax.dot_general(
-                cv_all[b, core], c_ref[...], (((1,), (1,)), ((), ())), preferred_element_type=F32
-            )
-        return carry
-
-    lax.fori_loop(0, nz, multiply, 0)
-    others(lambda *at: products(*at).start())
-    k2_all[plane, z, s] = k2_out[z, s]
+    def multiply(which, c_rows):
+        def body(b, carry):
+            for core in range(2):
+                k2_out[which, b, core] = lax.dot_general(
+                    cv_all[b, core], c_rows[...], (((1,), (1,)), ((), ())), preferred_element_type=F32
+                )
+            return carry
+
+        lax.fori_loop(0, nz, body, 0)
+        others(lambda *at: products(which, *at).start())
+        k2_all[plane, (z, end)[which], s] = k2_out[which, z, s]
 
     piece = width // PIECES
 
@@ -242,15 +274,55 @@
         h_line.got(b)
         use(b, mate)
 
+    def form_products():
+        @pl.when(inner)
+        def _():
+            def got(b, carry):
+                cv_line.got(b)
+                return carry
+
+            lax.fori_loop(0, nz, got, 0)
+            multiply(0, c_ref)
+
+        @pl.when(beside)
+        def _():
+            for copy in far_swaps():
+                copy.wait()
+            multiply(1, c_far)
+
     def h_step(t, carry):
+        cv_line.relay(t)
+
         @pl.when(t == nz - 1)
         def _():
-            others(lambda *at: products(*at).wait())
+            def arrive(step, b, core):
+                formed_here = (core == s) & beside & (b == end)
+
+                @pl.when(jnp.logical_not(formed_here))
+                def _():
+                    product_landed(step, b, core)
+
+            others(arrive)
+
+            @pl.when(jnp.logical_not(inner))
+            def _():
+                product_landed(0, z, s)
+
             others(lambda *at: columns(*at).wait())
             for copy in swaps():
                 copy.start()
 
         h_line.relay(t)
+
+        @pl.when((t == 1) & beside)
+        def _():
+            far().wait_recv()
+            for copy in far_swaps():
+                copy.start()
+
+        @pl.when(t == nz - 2)
+        def _():
+            form_products()
 
         @pl.when(z - t >= 0)
         def _():
@@ -328,6 +400,18 @@
         return carry
 
     lax.fori_loop(0, PIECES, final, 0)
+    @pl.when(jnp.logical_not(inner))
+    def _():
+        far().wait_send()
+
+    @pl.when(inner)
+    def _():
+        others(lambda *at: products(0, *at).wait_send())
+
+    @pl.when(beside)
+    def _():
+        others(lambda *at: products(1, *at).wait_send())
+
     cv_line.finish()
     h_line.finish()
 
@@ -359,7 +443,8 @@
             pltpu.VMEM((width, 2 * nz * toks), BF16),
             pltpu.VMEM((2 * nz * toks, span), BF16),
             pltpu.VMEM((nz, 2, vals, toks), F32),
-            pltpu.VMEM((nz, 2, rows_v, toks), F32),
+            pltpu.VMEM((toks, D), BF16),
+            pltpu.VMEM((2, nz, 2, rows_v, toks), F32),
             pltpu.VMEM((planes, nz, 2, rows_v, toks), F32),
             pltpu.VMEM((2, 8, LANES), F32),
             pltpu.VMEM((nx, 8, LANES), F32),
@@ -367,7 +452,8 @@
             sem(nz, hp), sem(nz, hp), sem(nz, hp), sem(nz, hp), sem(nz, hp),
             sem(nz, vp), sem(nz, vp), sem(nz, vp), sem(nz, vp), sem(nz, vp),
             sem(2 * nz - 1), sem(2 * nz - 1), sem(max(nx - 1, 1)), sem(max(nx - 1, 1)),
-            sem(2 * nz - 1), sem(2 * nz - 1), sem(max(nx - 1, 1)), sem(max(nx - 1, 1)),
+            sem(2, 2 * nz - 1), sem(nz, 2), sem(max(nx - 1, 1)), sem(max(nx - 1, 1)),
+            sem(1), sem(1), sem(max(nx - 1, 1)), sem(max(nx - 1, 1)),
             sem(1), sem(1), sem(max(nx - 1, 1)), sem(max(nx - 1, 1)), sem(nz - 1), sem(nz - 1),
         ],
         compiler_params=pltpu.CompilerParams(

time: 125 us -> 119 us (0.952)
  Pallas kernels: 119 us -> 113 us
    pallas_call x1, Pallas kernels: 119 us -> 113 us  [shards(): pl.pallas_call(functools.partial(kernel, nz, nx), out_shape=(jax.ShapeDty...]
where the time goes in v3:
time: 119 us; the launch traced here: 118 us
  Pallas kernels  113 us (95%)
  local copies, waits for them, and re-layouts  4.63 us (4%)
  between operations  1.29 us (1%)
    pallas_call x1, Pallas kernels, shards(): pl.pallas_call(functools.partial(kernel, nz, nx), out_shape=(jax.ShapeDty...  113 us
    unnamed x4, local copies, waits for them, and re-layouts  4.63 us

profile of v3, /device:TPU:0, one launch (start us, length us, event | category | flops | bytes accessed | tf_op | source)
XLA Modules:
  0.0 118.5 jit_solution(10408503181386771610)
XLA Ops:
  1.3 112.6 %shard_map.86 = (bf16[3584,512]{1,0:T(8,128)(2,1)}, f32[1,16]{1,0:T(1,128)}) custom-call(bf16[64,3584]{1,0:T(8,128)(2,1)} %hv_ref.1, bf16[64,4096]{1,0:T(8,128)(2,1)} %cv_ref.1, s32[1]{0:T(128)S(6)} %copy.11.count_ref, bf16[128,3584]{1,0:T(8,128)(2,1)} %h_ref.1, bf16[128,4096]{1,0:T(8,128)(2,1)} %c_ref.1, s32[16]{0:T(128)} %len_ref.1, s32[16]{0:T(128)} %dev_ref.1), custom_call_target="tpu_custom_call" | custom-call | flops 4499999744 | bytes 20000000 | tf_op jit(solution)/shard_map/pallas_call | solution.py:430
  113.9 0.0 copy-start
  113.9 4.1 %copy.12 = bf16[3584,512]{1,0:T(8,128)(2,1)} copy(bf16[3584,512]{1,0:T(8,128)(2,1)} %get-tuple-element.8) | data formatting | bytes 7340032
  118.0 0.0 copy-done
  118.0 0.5 copy.13
Async XLA Ops:
  113.9 4.1 %copy-start = (f32[1,16]{1,0:T(1,128)S(1)}, f32[1,16]{1,0:T(1,128)}, u32[]{:S(2)}) copy-start(f32[1,16]{1,0:T(1,128)} %get-tuple-element.5) | copy-start | bytes 196

commit v4 on v3

--- a/solution.py
+++ b/solution.py
@@ -16,8 +16,9 @@
 
 
 def kernel(
-    nz, nx, hv_ref, cv_ref, count_ref, h_ref, c_ref, len_ref, dev_ref,
-    out_ref, weight_ref,
+    nz, nx, hv_src, cv_src, count_ref, h_src, c_src, len_ref, dev_ref,
+    out_hbm, weight_ref,
+    out_ref, left_sem, hv_ref, c_ref, fetched,
     h_all, cv_all, c_all, kept, turned, weighted, k1_all, c_far, k2_out, k2_all, near, across, along,
     h_right, h_left, h_recv, h_give, h_get,
     cv_right, cv_left, cv_recv, cv_give, cv_get,
@@ -29,13 +30,22 @@
     s = lax.axis_index("sub")
     mate = 1 - s
     span = c_all.shape[3]
-    toks, width = h_ref.shape
+    toks, width = h_src.shape
     vals = hv_ref.shape[0]
     planes, _, _, rows_v, _ = k2_all.shape
     plane = x if planes > 1 else 0
     rows_c = toks // nx
     seqs = len_ref.shape[0]
 
+    rows_here = pl.ds(pl.multiple_of(plane * rows_v, 16), rows_v)
+    fetches = [
+        pltpu.make_async_copy(cv_src.at[rows_here], cv_all.at[z, s], fetched.at[0]),
+        pltpu.make_async_copy(h_src, h_all.at[z, s], fetched.at[1]),
+        pltpu.make_async_copy(c_src, c_ref, fetched.at[2]),
+        pltpu.make_async_copy(hv_src, hv_ref, fetched.at[3]),
+    ]
+    for fetch in fetches:
+        fetch.start()
     barrier = pltpu.get_barrier_semaphore()
     for step in range(1, 2 * nz):
         other = lax.rem(z * 2 + s + step, 2 * nz)
@@ -43,8 +53,6 @@
     for step in range(1, nx):
         pl.semaphore_signal(barrier, inc=1, device_id={"tensor": lax.rem(x + step, nx)})
 
-    cv_all[z, s] = cv_ref[pl.ds(pl.multiple_of(plane * rows_v, 16), rows_v), :]
-    h_all[z, s] = h_ref[...]
     pl.semaphore_wait(barrier, 2 * nz - 1 + nx - 1)
 
     def hop(full, b, k, rows, send, recv, target):
@@ -208,15 +216,20 @@
                 ))
         return copies
 
+    fetches[0].wait()
+    cv_line.begin()
+    fetches[1].wait()
+    h_line.begin()
+    fetches[2].wait()
+
     @pl.when(jnp.logical_not(inner))
     def _():
         far().start()
 
-    cv_line.begin()
-    h_line.begin()
     others(lambda *at: columns(*at).start())
     own = pl.ds(pl.multiple_of((z * 2 + s) * span, span), span)
     c_all[z, s, part] = c_ref[part, own]
+    fetches[3].wait()
     live = lax.broadcasted_iota(jnp.int32, hv_ref.shape, 0) < count_ref[0]
     kept[...] = jnp.where(live, hv_ref[...], jnp.zeros_like(hv_ref))
 
@@ -397,9 +410,17 @@
         at = pl.ds(pl.multiple_of(i * piece, LANES), piece)
         product = jnp.dot(turned[at, :], weighted[...], preferred_element_type=F32)
         out_ref[at, :] = (product / root).astype(BF16)
+        pltpu.make_async_copy(out_ref.at[at], out_hbm.at[at], left_sem.at[i]).start()
         return carry
 
     lax.fori_loop(0, PIECES, final, 0)
+
+    def left(i, carry):
+        at = pl.ds(pl.multiple_of(i * piece, LANES), piece)
+        pltpu.make_async_copy(out_ref.at[at], out_hbm.at[at], left_sem.at[i]).wait()
+        return carry
+
+    lax.fori_loop(0, PIECES, left, 0)
     @pl.when(jnp.logical_not(inner))
     def _():
         far().wait_send()
@@ -426,6 +447,7 @@
     sem = lambda *shape: pltpu.SemaphoreType.DMA(shape)
     hp, vp = (4, 2) if nz <= 4 else (1, 1)
     vmem = pl.BlockSpec(memory_space=pltpu.VMEM)
+    hbm = pl.BlockSpec(memory_space=pl.ANY)
     smem = pl.BlockSpec(memory_space=pltpu.SMEM)
     out, weight = pl.pallas_call(
         functools.partial(kernel, nz, nx),
@@ -433,9 +455,11 @@
             jax.ShapeDtypeStruct((width, span), BF16),
             jax.ShapeDtypeStruct((1, seqs), F32),
         ),
-        in_specs=[vmem, vmem, smem, vmem, vmem, smem, smem],
-        out_specs=(vmem, vmem),
+        in_specs=[hbm, hbm, smem, hbm, hbm, smem, smem],
+        out_specs=(hbm, vmem),
         scratch_shapes=[
+            pltpu.VMEM((width, span), BF16), sem(PIECES),
+            pltpu.VMEM((vals, width), BF16), pltpu.VMEM((toks, D), BF16), sem(4),
             pltpu.VMEM((nz, 2, toks, width), BF16),
             pltpu.VMEM((nz, 2, rows_v, D), BF16),
             pltpu.VMEM((nz, 2, toks, span), BF16),

time: 119 us -> 117 us (0.983)
  Pallas kernels: 113 us -> 111 us
    pallas_call x1, Pallas kernels: 113 us -> 111 us  [shards(): pl.pallas_call(functools.partial(kernel, nz, nx), out_shape=(jax.ShapeDty...]
where the time goes in v4:
time: 117 us
  Pallas kernels  111 us (95%)
  local copies, waits for them, and re-layouts  4.63 us (4%)
  between operations  1.29 us (1%)
    pallas_call x1, Pallas kernels, shards(): pl.pallas_call(functools.partial(kernel, nz, nx), out_shape=(jax.ShapeDty...  111 us
    unnamed x4, local copies, waits for them, and re-layouts  4.63 us

profile of v4, /device:TPU:0, one launch (start us, length us, event | category | flops | bytes accessed | tf_op | source)
XLA Modules:
  0.0 116.9 jit_solution(2356308891610868276)
XLA Ops:
  1.3 111.0 %shard_map.86 = (bf16[3584,512]{1,0:T(8,128)(2,1)}, f32[1,16]{1,0:T(1,128)}) custom-call(bf16[64,3584]{1,0:T(8,128)(2,1)} %hv_src.1, bf16[64,4096]{1,0:T(8,128)(2,1)} %cv_src.1, s32[1]{0:T(128)S(6)} %copy.11.count_ref, bf16[128,3584]{1,0:T(8,128)(2,1)} %h_src.1, bf16[128,4096]{1,0:T(8,128)(2,1)} %c_src.1, s32[16]{0:T(128)} %len_ref.1, s32[16]{0:T(128)} %dev_ref.1), custom_call_target="tpu_custom_call" | custom-call | flops 4499999744 | bytes 20000000 | tf_op jit(solution)/shard_map/pallas_call | solution.py:452
  112.3 0.0 copy-start
  112.3 4.1 %copy.12 = bf16[3584,512]{1,0:T(8,128)(2,1)} copy(bf16[3584,512]{1,0:T(8,128)(2,1)} %get-tuple-element.8) | data formatting | bytes 7340032
  116.4 0.0 copy-done
  116.4 0.5 copy.13
Async XLA Ops:
  112.3 4.1 %copy-start = (f32[1,16]{1,0:T(1,128)S(1)}, f32[1,16]{1,0:T(1,128)}, u32[]{:S(2)}) copy-start(f32[1,16]{1,0:T(1,128)} %get-tuple-element.5) | copy-start | bytes 196
